TPU v7x, 1024 devices: a whole 4x4x32 slice. The times are simulated.
1024 devices in a mesh: row: 32 (over x, z_hi, y), col: 16 (over z_lo), layer: 2 (over core).
Axes of the slice: x: 4, y: 4, z: 32 (z_hi: 2, z_lo: 16; z = z_hi * 16 + z_lo), core: 2. Of those that a mesh axis runs over, the one named last changes fastest.
Arguments:
- left_panels: bfloat16 [32, 16, 2, 32, 128, 128], P('row', 'col', 'layer'), may hold values from -6 to 6
- right_panels: bfloat16 [32, 16, 2, 32, 128, 128], P('row', 'col', 'layer'), may hold values from -0.09375 to 0.09375
- left_picks: int32 [32, 16, 2, 4, 16, 4], P('row', 'col', 'layer'), may hold values from 0 to 31
- right_picks: int32 [32, 16, 2, 4, 16, 4], P('row', 'col', 'layer'), may hold values from 0 to 31
- live_count: int32 [32, 16, 2, 4, 16], P('row', 'col', 'layer'), may hold values from 0 to 4, as said below
Outputs:
- product_blocks: float32 [32, 16, 16, 128, 128], P('row', 'col', 'layer')
Inputs may be any that keep to these rules, and one draw needn't show every extreme that they name: live_count[r, c, l, s, j] counts the leading pairs q < live_count of product block j that take part at step s; the value 4 occurs in every draw.
All inputs are finite; a program needn't handle non-finite values.
Results may differ from a plain program's by a relative error of at most 0.0003.
Values may be sent and summed in bfloat16 or wider, within the bound.
A program may use at most 32 MiB of HBM per device.

v0:
```python
import jax
import jax.numpy as jnp
from jax import lax
from jax.sharding import PartitionSpec as P

STEPS = 4


def shifted(value, axis, steps):
    count = lax.axis_size(axis)
    pairs = [(source, (source + steps) % count) for source in range(count)]
    return lax.ppermute(value, axis, pairs)


def select_blocks(panel, picks, active):
    padded = jnp.concatenate([panel, jnp.zeros((1,) + panel.shape[1:], panel.dtype)], axis=0)
    chosen = jnp.where(active, picks, jnp.int32(panel.shape[0]))
    return padded[chosen]


def block_step(left_panel, right_panel, left_list, right_list, counts):
    active = jnp.arange(left_list.shape[-1], dtype=jnp.int32)[None, :] < counts[:, None]
    left_sel = select_blocks(left_panel, left_list, active)
    right_sel = select_blocks(right_panel, right_list, active)
    return jnp.einsum("cqik,cqkj->cij", left_sel, right_sel, preferred_element_type=jnp.float32)


def local(left_panels, right_panels, left_picks, right_picks, live_count):
    left_home = left_panels[0, 0, 0]
    right_home = right_panels[0, 0, 0]
    left_lists = left_picks[0, 0, 0]
    right_lists = right_picks[0, 0, 0]
    counts_all = live_count[0, 0, 0]
    width = left_home.shape[-1]
    totals = jnp.zeros((counts_all.shape[-1], width, width), jnp.float32)
    left_panel = left_home
    right_panel = right_home
    for step in range(STEPS):
        if step > 0:
            left_panel = shifted(left_panel, "col", -1)
            right_panel = shifted(right_panel, "row", -1)
        totals = totals + block_step(
            left_panel, right_panel, left_lists[step], right_lists[step], counts_all[step]
        )
    summed = lax.psum_scatter(totals, "layer", scatter_dimension=0, tiled=True)
    return summed[None, None]


def solution(mesh):
    placed = (
        P("row", "col", "layer", None, None, None),
        P("row", "col", "layer", None, None, None),
        P("row", "col", "layer", None, None, None),
        P("row", "col", "layer", None, None, None),
        P("row", "col", "layer", None, None),
    )
    return jax.shard_map(
        local,
        mesh=mesh,
        in_specs=placed,
        out_specs=P("row", "col", "layer", None, None),
        check_vma=False,
    )
```

profile of v0, /device:TPU:1, one launch (start us, length us, event | category | flops | bytes accessed | tf_op | source)
XLA Modules:
  0.0 715.4 jit_solution(1794064853239110260)
XLA Ops:
  6.5 27.1 %collective-permute-start = (bf16[32,128,128]{2,1,0:T(8,128)(2,1)}, bf16[32,128,128]{2,1,0:T(8,128)(2,1)}, u32[]{:S(2)}, u32[]{:S(2)}) collective-permute-start(bf16[32,128,128]{2,1,0:T(8,128)(2,1)} %bitcast.101), channel_id=1, source_target_pairs={{0,30},{2,0},{4,2},{6,4},{8,6},{10,8},{12,10},{14,12},{16,14},{18,... | collective-permute-start | bytes 3145736 | tf_op jit(solution)/shard_map/ppermute | solution.py:12
  33.7 16.4 %collective-permute-start.1 = (bf16[32,128,128]{2,1,0:T(8,128)(2,1)}, bf16[32,128,128]{2,1,0:T(8,128)(2,1)}, u32[]{:S(2)}, u32[]{:S(2)}) collective-permute-start(bf16[32,128,128]{2,1,0:T(8,128)(2,1)} %bitcast.103), channel_id=1, source_target_pairs={{0,992},{32,0},{64,32},{96,64},{128,96},{160,128},{192,160},{224,1... | collective-permute-start | bytes 3145736 | tf_op jit(solution)/shard_map/ppermute | solution.py:12
  50.0 1.3 concatenate.25
  51.5 20.0 %collective-permute-done = bf16[32,128,128]{2,1,0:T(8,128)(2,1)} collective-permute-done((bf16[32,128,128]{2,1,0:T(8,128)(2,1)}, bf16[32,128,128]{2,1,0:T(8,128)(2,1)}, u32[]{:S(2)}, u32[]{:S(2)}) %collective-permute-start) | collective-permute-done | bytes 1048608 | tf_op jit(solution)/shard_map/ppermute | solution.py:12
  71.5 20.6 %collective-permute-start.2 = (bf16[32,128,128]{2,1,0:T(8,128)(2,1)}, bf16[32,128,128]{2,1,0:T(8,128)(2,1)}, u32[]{:S(2)}, u32[]{:S(2)}) collective-permute-start(bf16[32,128,128]{2,1,0:T(8,128)(2,1)} %collective-permute-done), channel_id=1, source_target_pairs={{0,30},{2,0},{4,2},{6,4},{8,6},{10,8},{12,10},{14,12},{16,14},{18,... | collective-permute-start | bytes 3145736 | tf_op jit(solution)/shard_map/ppermute | solution.py:12
  92.1 19.3 %collective-permute-done.1 = bf16[32,128,128]{2,1,0:T(8,128)(2,1)} collective-permute-done((bf16[32,128,128]{2,1,0:T(8,128)(2,1)}, bf16[32,128,128]{2,1,0:T(8,128)(2,1)}, u32[]{:S(2)}, u32[]{:S(2)}) %collective-permute-start.1) | collective-permute-done | bytes 1048608 | tf_op jit(solution)/shard_map/ppermute | solution.py:12
  111.4 27.1 %collective-permute-start.3 = (bf16[32,128,128]{2,1,0:T(8,128)(2,1)}, bf16[32,128,128]{2,1,0:T(8,128)(2,1)}, u32[]{:S(2)}, u32[]{:S(2)}) collective-permute-start(bf16[32,128,128]{2,1,0:T(8,128)(2,1)} %collective-permute-done.1), channel_id=1, source_target_pairs={{0,992},{32,0},{64,32},{96,64},{128,96},{160,128},{192,160},{224,1... | collective-permute-start | bytes 3145736 | tf_op jit(solution)/shard_map/ppermute | solution.py:12
  140.1 2.1 gather_fusion.1
  142.2 2.1 gather_fusion
  144.4 103.9 %collective-permute-done.2 = bf16[32,128,128]{2,1,0:T(8,128)(2,1)} collective-permute-done((bf16[32,128,128]{2,1,0:T(8,128)(2,1)}, bf16[32,128,128]{2,1,0:T(8,128)(2,1)}, u32[]{:S(2)}, u32[]{:S(2)}) %collective-permute-start.2) | collective-permute-done | bytes 1048608 | tf_op jit(solution)/shard_map/ppermute | solution.py:12
  248.3 11.8 %collective-permute-start.4 = (bf16[32,128,128]{2,1,0:T(8,128)(2,1)}, bf16[32,128,128]{2,1,0:T(8,128)(2,1)}, u32[]{:S(2)}, u32[]{:S(2)}) collective-permute-start(bf16[32,128,128]{2,1,0:T(8,128)(2,1)} %collective-permute-done.2), channel_id=1, source_target_pairs={{0,30},{2,0},{4,2},{6,4},{8,6},{10,8},{12,10},{14,12},{16,14},{18,... | collective-permute-start | bytes 3145736 | tf_op jit(solution)/shard_map/ppermute | solution.py:12
  260.2 1.9 collective-permute-start.5
  262.1 3.3 convolution_bitcast_fusion.3
  267.7 1.3 concatenate.27
  269.0 2.1 gather_fusion.3
  271.1 3.5 fusion
  276.9 1.3 concatenate.29
  278.3 2.1 gather_fusion.5
  280.4 3.5 fusion.1
  283.9 183.7 %collective-permute-done.4 = bf16[32,128,128]{2,1,0:T(8,128)(2,1)} collective-permute-done((bf16[32,128,128]{2,1,0:T(8,128)(2,1)}, bf16[32,128,128]{2,1,0:T(8,128)(2,1)}, u32[]{:S(2)}, u32[]{:S(2)}) %collective-permute-start.4) | collective-permute-done | bytes 1048608 | tf_op jit(solution)/shard_map/ppermute | solution.py:12
  470.0 1.3 concatenate.31
  471.3 2.1 gather_fusion.7
  473.4 3.5 fusion.2
  477.0 231.6 %reduce-scatter.2.cloned.1.call-done = f32[8,128,128]{2,1,0:T(8,128)} async-done(((f32[16,128,128]{2,1,0:T(8,128)}), f32[8,128,128]{2,1,0:T(8,128)}) %reduce-scatter.2.cloned.1.call-update) | async-done | bytes 524304 | tf_op jit(solution)/shard_map/reduce_scatter | solution.py:45
  (47 shorter events, 8.4 us)
Async XLA Ops:
  6.5 44.8 %copy-start.1 = (bf16[1,1,1,32,128,128]{5,4,3,2,1,0:T(8,128)(2,1)S(1)}, bf16[1,1,1,32,128,128]{5,4,3,2,1,0:T(8,128)(2,1)}, u32[]{:S(2)}) copy-start(bf16[1,1,1,32,128,128]{5,4,3,2,1,0:T(8,128)(2,1)} %param.5) | copy-start | bytes 3145732
  6.5 702.0 %reduce-scatter.2.cloned.1.call-start = ((), (), s32[]{:S(2)}) async-start(), calls=%async_computation.1 | async-start | bytes 1572864 | tf_op jit(solution)/shard_map/reduce_scatter | solution.py:45
  6.5 64.9 %collective-permute-start = (bf16[32,128,128]{2,1,0:T(8,128)(2,1)}, bf16[32,128,128]{2,1,0:T(8,128)(2,1)}, u32[]{:S(2)}, u32[]{:S(2)}) collective-permute-start(bf16[32,128,128]{2,1,0:T(8,128)(2,1)} %bitcast.101), channel_id=1, source_target_pairs={{0,30},{2,0},{4,2},{6,4},{8,6},{10,8},{12,10},{14,12},{16,14},{18,... | collective-permute-start | bytes 3145736 | tf_op jit(solution)/shard_map/ppermute | solution.py:12
  33.6 17.9 %copy-start.4 = (s32[1,1,1,4,16]{4,3,2,1,0:T(4,128)S(1)}, s32[1,1,1,4,16]{4,3,2,1,0:T(4,128)}, u32[]{:S(2)}) copy-start(s32[1,1,1,4,16]{4,3,2,1,0:T(4,128)} %param.9) | copy-start | bytes 772
  33.6 105.0 %copy-start.2 = (s32[1,1,1,4,16,4]{4,5,3,2,1,0:T(4,128)S(1)}, s32[1,1,1,4,16,4]{4,5,3,2,1,0:T(4,128)}, u32[]{:S(2)}) copy-start(s32[1,1,1,4,16,4]{4,5,3,2,1,0:T(4,128)} %param.7) | copy-start | bytes 3076
  33.6 105.0 %copy-start.3 = (s32[1,1,1,4,16,4]{4,5,3,2,1,0:T(4,128)S(1)}, s32[1,1,1,4,16,4]{4,5,3,2,1,0:T(4,128)}, u32[]{:S(2)}) copy-start(s32[1,1,1,4,16,4]{4,5,3,2,1,0:T(4,128)} %param.8) | copy-start | bytes 3076
  33.7 77.8 %collective-permute-start.1 = (bf16[32,128,128]{2,1,0:T(8,128)(2,1)}, bf16[32,128,128]{2,1,0:T(8,128)(2,1)}, u32[]{:S(2)}, u32[]{:S(2)}) collective-permute-start(bf16[32,128,128]{2,1,0:T(8,128)(2,1)} %bitcast.103), channel_id=1, source_target_pairs={{0,992},{32,0},{64,32},{96,64},{128,96},{160,128},{192,160},{224,1... | collective-permute-start | bytes 3145736 | tf_op jit(solution)/shard_map/ppermute | solution.py:12
  71.5 176.8 %collective-permute-start.2 = (bf16[32,128,128]{2,1,0:T(8,128)(2,1)}, bf16[32,128,128]{2,1,0:T(8,128)(2,1)}, u32[]{:S(2)}, u32[]{:S(2)}) collective-permute-start(bf16[32,128,128]{2,1,0:T(8,128)(2,1)} %collective-permute-done), channel_id=1, source_target_pairs={{0,30},{2,0},{4,2},{6,4},{8,6},{10,8},{12,10},{14,12},{16,14},{18,... | collective-permute-start | bytes 3145736 | tf_op jit(solution)/shard_map/ppermute | solution.py:12
  111.4 148.7 %collective-permute-start.3 = (bf16[32,128,128]{2,1,0:T(8,128)(2,1)}, bf16[32,128,128]{2,1,0:T(8,128)(2,1)}, u32[]{:S(2)}, u32[]{:S(2)}) collective-permute-start(bf16[32,128,128]{2,1,0:T(8,128)(2,1)} %collective-permute-done.1), channel_id=1, source_target_pairs={{0,992},{32,0},{64,32},{96,64},{128,96},{160,128},{192,160},{224,1... | collective-permute-start | bytes 3145736 | tf_op jit(solution)/shard_map/ppermute | solution.py:12
  142.2 119.9 %copy-start = (bf16[64,128,128]{2,1,0:T(8,128)(2,1)S(1)}, bf16[64,128,128]{2,1,0:T(8,128)(2,1)}, u32[]{:S(2)}) copy-start(bf16[64,128,128]{2,1,0:T(8,128)(2,1)} %gather_fusion.1) | copy-start | bytes 6291460
  248.3 219.4 %collective-permute-start.4 = (bf16[32,128,128]{2,1,0:T(8,128)(2,1)}, bf16[32,128,128]{2,1,0:T(8,128)(2,1)}, u32[]{:S(2)}, u32[]{:S(2)}) collective-permute-start(bf16[32,128,128]{2,1,0:T(8,128)(2,1)} %collective-permute-done.2), channel_id=1, source_target_pairs={{0,30},{2,0},{4,2},{6,4},{8,6},{10,8},{12,10},{14,12},{16,14},{18,... | collective-permute-start | bytes 3145736 | tf_op jit(solution)/shard_map/ppermute | solution.py:12
  260.2 209.8 %collective-permute-start.5 = (bf16[32,128,128]{2,1,0:T(8,128)(2,1)}, bf16[32,128,128]{2,1,0:T(8,128)(2,1)}, u32[]{:S(2)}, u32[]{:S(2)}) collective-permute-start(bf16[32,128,128]{2,1,0:T(8,128)(2,1)} %collective-permute-done.3), channel_id=1, source_target_pairs={{0,992},{32,0},{64,32},{96,64},{128,96},{160,128},{192,160},{224,1... | collective-permute-start | bytes 3145736 | tf_op jit(solution)/shard_map/ppermute | solution.py:12
Sparse Core Ops, SparseCore 0:
  477.1 231.3 reduce-scatter.1
where the time goes:
time: 716 us; the launch traced here: 715 us
  waiting for transfers between devices  559 us (78%)
  starting transfers between devices  105 us (15%)
  local copies, waits for them, and re-layouts  24.3 us (3%)
  matrix products  13.8 us (2%)
  between operations  13.7 us (2%)
    ppermute x6, waiting for transfers between devices, shifted(): return lax.ppermute(value, axis, pairs)  327 us
    reduce_scatter x1, waiting for transfers between devices, local(): summed = lax.psum_scatter(totals, 'layer', scatter_dimension=0, tiled=True)  232 us
    ppermute x6, starting transfers between devices, shifted(): return lax.ppermute(value, axis, pairs)  105 us
  transfers between devices with their start and end apart: 7, of which 5 were waited for; matrix products, arithmetic and copies ran while one was open for 4% of the time, Pallas kernels for 0%

commit v1 on v0

v1 whole, which is shorter than its diff:
```python
import functools

import jax
import jax.numpy as jnp
from jax import lax
from jax.experimental import pallas as pl
from jax.experimental.pallas import tpu as pltpu
from jax.sharding import PartitionSpec as P

MESH = pl.DeviceIdType.MESH

STEPS = 4
NY = 4
BS = 128
CAP = 32
CB = 16
Q = 4
CHUNKS = 3
LANE = 4
LEFT = 2


def kernel(
    nx, nc,
    lp_ref, rp_ref, live_ref, left_hbm, right_hbm, out_ref,
    lown, rown, lbuf, rbuf, lane, totals, partner,
    own_sem, lane_send, lane_recv, left_send, left_recv, wrap_send,
    seed_send, seed_recv, near_send, right_recv, spread_send, sum_send, sum_recv,
):
    hops = nc
    items = hops * CHUNKS
    lag = CAP // LEFT
    row = lax.axis_index("row")
    c = lax.axis_index("col")
    l = lax.axis_index("layer")
    x = row // (2 * NY)
    h = (row // NY) % 2
    y = row % NY

    def at(px, ph, py, pc, pll):
        return (px * (2 * NY) + ph * NY + py, pc, pll)

    def ring(px):
        return lax.rem(px + nx, nx)

    first, last = c == 0, c == nc - 1
    up_c = jnp.where(last, 0, c + 1)
    down_c = jnp.where(first, nc - 1, c - 1)
    up_h = jnp.where(last, 1 - h, h)
    down_h = jnp.where(first, 1 - h, h)
    up_next = at(ring(x - jnp.where(last & (h == 0), 1, 0)), up_h, y, up_c, l)
    up_prev = at(ring(x + jnp.where(first & (h == 1), 1, 0)), down_h, y, down_c, l)
    down_next = at(ring(x - jnp.where(first & (h == 0), 1, 0)), down_h, y, down_c, l)
    down_prev = at(ring(x + jnp.where(last & (h == 1), 1, 0)), up_h, y, up_c, l)
    nexts = (up_next, down_next)

    def in_group(py):
        return at(x, h, py, c, l)

    def on_col(pc):
        return at(x, h, y, pc, l)

    sibling = at(x, h, y, c, 1 - l)

    own_left = pltpu.make_async_copy(left_hbm, lown.at[pl.ds(0, CAP)], own_sem.at[0])
    own_right = pltpu.make_async_copy(right_hbm, rown, own_sem.at[1])
    own_left.start()
    own_right.start()

    def own_lane(d):
        return pltpu.make_async_copy(
            right_hbm.at[pl.ds(d * CHUNKS * LANE, CHUNKS * LANE)],
            lane.at[d, pl.ds(0, CHUNKS * LANE)],
            own_sem.at[2 + d],
        )

    @pl.when(y < NY - 1)
    def _():
        own_lane(0).start()
        own_lane(1).start()

    lown[CAP] = jnp.zeros((BS, BS), lown.dtype)
    lbuf[(STEPS - 1) * CAP] = jnp.zeros((BS, BS), lbuf.dtype)

    barrier = pltpu.get_barrier_semaphore()
    for who in (up_prev, down_prev, sibling):
        pl.semaphore_signal(barrier, inc=1, device_id=who, device_id_type=MESH)
    for k in range(1, NY):
        pl.semaphore_signal(
            barrier, inc=1, device_id=in_group(lax.rem(y + k, NY)), device_id_type=MESH
        )

    @pl.when(c < nc - 1)
    def _():
        pl.semaphore_signal(barrier, inc=1, device_id=on_col(c + 1), device_id_type=MESH)

    @pl.when(last)
    def _():
        for k in range(STEPS - 1):
            pl.semaphore_signal(barrier, inc=1, device_id=on_col(k), device_id_type=MESH)

    greeted = 3 + (NY - 1) + jnp.where(c > 0, 1, 0) + jnp.where(c < STEPS - 1, 1, 0)
    pl.semaphore_wait(barrier, greeted)

    spare = 2 * CHUNKS * LANE

    def seed(d, who):
        return pltpu.make_async_remote_copy(
            src_ref=right_hbm.at[pl.ds(spare + d * LANE, LANE)],
            dst_ref=lane.at[d, pl.ds(who * LANE, LANE)],
            send_sem=seed_send.at[d],
            recv_sem=seed_recv.at[d, who],
            device_id=in_group(NY - 1),
            device_id_type=MESH,
        )

    @pl.when(y < NY - 1)
    def _():
        seed(0, y).start()
        seed(1, y).start()
        own_lane(0).wait()
        own_lane(1).wait()

    own_left.wait()
    own_right.wait()

    def lane_copy(d, it):
        return pltpu.make_async_remote_copy(
            src_ref=lane.at[d, pl.ds(it * LANE, LANE)],
            dst_ref=lane.at[d, pl.ds((it + CHUNKS) * LANE, LANE)],
            send_sem=lane_send.at[d, it],
            recv_sem=lane_recv.at[d, it],
            device_id=nexts[d],
            device_id_type=MESH,
        )

    def left_copy(it, src=None):
        if src is None:
            src = lbuf.at[pl.ds(it * LEFT, LEFT)]
        return pltpu.make_async_remote_copy(
            src_ref=src,
            dst_ref=lbuf.at[pl.ds(it * LEFT, LEFT)],
            send_sem=left_send.at[it],
            recv_sem=left_recv.at[it],
            device_id=on_col(jnp.maximum(c - 1, 0)),
            device_id_type=MESH,
        )

    def wrap_copy(it):
        return pltpu.make_async_remote_copy(
            src_ref=lown.at[pl.ds(lax.rem(it, lag) * LEFT, LEFT)],
            dst_ref=lbuf.at[pl.ds(it * LEFT, LEFT)],
            send_sem=wrap_send.at[lax.rem(it, lag)],
            recv_sem=left_recv.at[it],
            device_id=on_col(nc - 1),
            device_id_type=MESH,
        )

    near = 4
    near_copies = CAP // near

    def near_copy(s, k):
        return pltpu.make_async_remote_copy(
            src_ref=rown.at[pl.ds(k * near, near)],
            dst_ref=rbuf.at[pl.ds((s - 1) * CAP + k * near, near)],
            send_sem=near_send.at[s - 1, k],
            recv_sem=right_recv.at[s - 1],
            device_id=in_group(jnp.maximum(y - s, 0)),
            device_id_type=MESH,
        )

    def pair_sum(j, s):
        lefts, rights = [], []
        for q in range(Q):
            index = (s * CB + j) * Q + q
            used = q < live_ref[s * CB + j]
            if s == 0:
                lefts.append(lown[jnp.where(used, lp_ref[index], CAP)])
                rights.append(rown[rp_ref[index]])
            else:
                base = (s - 1) * CAP
                lefts.append(lbuf[jnp.where(used, base + lp_ref[index], (STEPS - 1) * CAP)])
                rights.append(rbuf[base + rp_ref[index]])
        return jnp.dot(
            jnp.concatenate(lefts, axis=1),
            jnp.concatenate(rights, axis=0),
            preferred_element_type=jnp.float32,
        )

    def step(it, _):
        @pl.when(it >= CHUNKS)
        def _():
            for d in range(2):
                lane_copy(d, it - CHUNKS).wait_recv()

        @pl.when((it < CHUNKS) & (y == NY - 1))
        def _():
            for d in range(2):
                seed(d, it).wait_recv()

        for d in range(2):
            lane_copy(d, it).start()

        @pl.when(it >= lag)
        def _():
            left_copy(it - lag).wait_recv()

        @pl.when((c > 0) & (it < lag))
        def _():
            left_copy(it, lown.at[pl.ds(it * LEFT, LEFT)]).start()

        @pl.when((c > 0) & (it >= lag))
        def _():
            left_copy(it, lbuf.at[pl.ds((it - lag) * LEFT, LEFT)]).start()

        @pl.when(it // lag == c)
        def _():
            wrap_copy(it).start()

        @pl.when((it >= CHUNKS) & (it < CHUNKS + near_copies))
        def _():
            for s in range(1, STEPS):

                @pl.when(y >= s)
                def _():
                    near_copy(s, it - CHUNKS).start()

        @pl.when(lax.rem(it, CHUNKS) == 2)
        def _():
            j = it // CHUNKS
            totals[j] = pair_sum(j, 0)

        return 0

    lax.fori_loop(0, items, step, 0)

    def spread(d, ch, to):
        src = jnp.where(y < NY - 1, y, ch)
        block = jnp.where(y < NY - 1, (d * CHUNKS + ch) * LANE, spare + d * LANE)
        start = (NY + src - to - 1) * CAP + block
        return src, start

    def spread_copy(d, ch, to):
        src, start = spread(d, ch, to)
        return pltpu.make_async_remote_copy(
            src_ref=lane.at[d, pl.ds((items + ch) * LANE, LANE)],
            dst_ref=rbuf.at[pl.ds(start, LANE)],
            send_sem=spread_send.at[d, ch, to - 1],
            recv_sem=right_recv.at[NY + src - to - 1],
            device_id=in_group(to),
            device_id_type=MESH,
        )

    def spread_here(d, ch):
        src, start = spread(d, ch, NY - 1)
        return pltpu.make_async_copy(
            lane.at[d, pl.ds((items + ch) * LANE, LANE)],
            rbuf.at[pl.ds(start, LANE)],
            right_recv.at[src],
        )

    for ch in range(CHUNKS):
        for d in range(2):
            lane_copy(d, items - CHUNKS + ch).wait_recv()
            for to in range(1, NY):
                src, _ = spread(d, ch, to)

                @pl.when((to > src) & (to != y))
                def _():
                    spread_copy(d, ch, to).start()

            @pl.when(y == NY - 1)
            def _():
                spread_here(d, ch).start()

    lax.fori_loop(items - lag, items, lambda it, _: (left_copy(it).wait_recv(), 0)[1], 0)
    for s in range(1, STEPS):
        panel = rbuf.at[pl.ds((s - 1) * CAP, CAP)]
        pltpu.make_async_copy(panel, panel, right_recv.at[s - 1]).wait()

    half = CB // 2

    def rest(j):
        total = totals[j]
        for s in range(1, STEPS):
            total = total + pair_sum(j, s)
        return total

    def sum_copy(i):
        return pltpu.make_async_remote_copy(
            src_ref=totals.at[(1 - l) * half + i],
            dst_ref=partner.at[i],
            send_sem=sum_send.at[i],
            recv_sem=sum_recv.at[i],
            device_id=sibling,
            device_id_type=MESH,
        )

    def theirs(i, _):
        j = (1 - l) * half + i
        totals[j] = rest(j)
        sum_copy(i).start()
        return 0

    def ours(i, _):
        out_ref[i] = rest(l * half + i)
        return 0

    lax.fori_loop(0, half, theirs, 0)
    lax.fori_loop(0, half, ours, 0)

    def lanes_gone(it, _):
        for d in range(2):
            lane_copy(d, it).wait_send()

        @pl.when(c > 0)
        def _():
            left_copy(it).wait_send()

        @pl.when(it // lag == c)
        def _():
            wrap_copy(it).wait_send()

        return 0

    lax.fori_loop(0, items, lanes_gone, 0)

    @pl.when(y < NY - 1)
    def _():
        seed(0, y).wait_send()
        seed(1, y).wait_send()

    for s in range(1, STEPS):

        @pl.when(y >= s)
        def _():
            lax.fori_loop(0, near_copies, lambda k, _: (near_copy(s, k).wait_send(), 0)[1], 0)

    for ch in range(CHUNKS):
        for d in range(2):
            for to in range(1, NY):
                src, _ = spread(d, ch, to)

                @pl.when((to > src) & (to != y))
                def _():
                    spread_copy(d, ch, to).wait_send()

    def finish(i, _):
        sum_copy(i).wait_recv()
        out_ref[i] = out_ref[i] + partner[i]
        sum_copy(i).wait_send()
        return 0

    lax.fori_loop(0, half, finish, 0)


def solution(mesh):
    nx = mesh.shape["row"] // (2 * NY)
    nc = mesh.shape["col"]
    items = nc * CHUNKS
    dma = pltpu.SemaphoreType.DMA

    def local(left_panels, right_panels, left_picks, right_picks, live_count):
        summed = pl.pallas_call(
            functools.partial(kernel, nx, nc),
            out_shape=jax.ShapeDtypeStruct((CB // 2, BS, BS), jnp.float32),
            in_specs=[pl.BlockSpec(memory_space=pltpu.SMEM)] * 3
            + [pl.BlockSpec(memory_space=pl.ANY)] * 2,
            out_specs=pl.BlockSpec(memory_space=pltpu.VMEM),
            scratch_shapes=[
                pltpu.VMEM((CAP + 1, BS, BS), jnp.bfloat16),
                pltpu.VMEM((CAP, BS, BS), jnp.bfloat16),
                pltpu.VMEM(((STEPS - 1) * CAP + 1, BS, BS), jnp.bfloat16),
                pltpu.VMEM(((STEPS - 1) * CAP, BS, BS), jnp.bfloat16),
                pltpu.VMEM((2, (items + CHUNKS) * LANE, BS, BS), jnp.bfloat16),
                pltpu.VMEM((CB, BS, BS), jnp.float32),
                pltpu.VMEM((CB // 2, BS, BS), jnp.float32),
                dma((4,)),
                dma((2, items)),
                dma((2, items)),
                dma((items,)),
                dma((items,)),
                dma((CAP // LEFT,)),
                dma((2,)),
                dma((2, CHUNKS)),
                dma((STEPS - 1, CAP // 4)),
                dma((STEPS - 1,)),
                dma((2, CHUNKS, NY - 1)),
                dma((CB // 2,)),
                dma((CB // 2,)),
            ],
            compiler_params=pltpu.CompilerParams(
                collective_id=0, has_side_effects=True, vmem_limit_bytes=48 * 2**20
            ),
            name="cannon_window",
        )(
            left_picks.reshape(-1),
            right_picks.reshape(-1),
            live_count.reshape(-1),
            left_panels[0, 0, 0],
            right_panels[0, 0, 0],
        )
        return summed[None, None]

    placed = (
        P("row", "col", "layer", None, None, None),
        P("row", "col", "layer", None, None, None),
        P("row", "col", "layer", None, None, None),
        P("row", "col", "layer", None, None, None),
        P("row", "col", "layer", None, None),
    )
    return jax.shard_map(
        local,
        mesh=mesh,
        in_specs=placed,
        out_specs=P("row", "col", "layer", None, None),
        check_vma=False,
    )
```

time: 716 us -> 266 us (0.37)
  the two profiles are of different devices: /device:TPU:1 before, /device:TPU:116 now
where the time goes in v1:
time: 266 us; the launch traced here: 265 us
  Pallas kernels  259 us (97%)
  local copies, waits for them, and re-layouts  5.69 us (2%)
    pallas_call x1, Pallas kernels, local(): pl.pallas_call(functools.partial(kernel, nx, nc), out_shape=jax.ShapeDtyp...  259 us
    unnamed x11, local copies, waits for them, and re-layouts  5.41 us

profile of v1, /device:TPU:116, one launch (start us, length us, event | category | flops | bytes accessed | tf_op | source)
XLA Modules:
  0.0 265.2 jit_solution(16117124659383827234)
XLA Ops:
  0.0 0.0 copy-start.3
  0.0 0.7 copy-done.3
  0.7 0.1 reshape.11.live_ref
  0.8 0.8 copy.6
  1.6 0.0 copy-start.2
  1.6 0.1 reshape.9.lp_ref
  1.7 0.6 copy-done.2
  2.3 0.1 copy.7
  2.4 0.1 reshape.10.rp_ref
  2.5 0.0 copy-start
  2.5 1.2 copy-done
  3.7 0.0 copy-start.1
  3.7 1.2 copy-done.1
  4.9 259.5 %cannon_window.1 = f32[8,128,128]{2,1,0:T(8,128)S(1)} custom-call(s32[256]{0:T(256)S(1)} %reshape.9.lp_ref, s32[256]{0:T(256)S(1)} %reshape.10.rp_ref, s32[64]{0:T(128)S(1)} %reshape.11.live_ref, bf16[32,128,128]{2,1,0:T(8,128)(2,1)S(1)} %bitcast.8, bf16[32,128,128]{2,1,0:T(8,128)(2,1)S(1)} %bitcast.9), custom_call_target="tpu_custom_call" | custom-call | tf_op jit(solution)/shard_map/cannon_window/pallas_call | solution.py:364
  264.4 0.8 copy.9
Async XLA Ops:
  0.0 0.7 copy-start.3
  1.6 0.7 copy-start.2
  2.5 1.2 copy-start
  3.7 1.2 copy-start.1

commit v2 on v1

--- a/solution.py
+++ b/solution.py
@@ -18,18 +18,20 @@
 CHUNKS = 3
 LANE = 4
 LEFT = 2
+LEAD = 8
 
 
 def kernel(
     nx, nc,
     lp_ref, rp_ref, live_ref, left_hbm, right_hbm, out_ref,
-    lown, rown, lbuf, rbuf, lane, totals, partner,
+    left0, left1, left2, left3, right0, right1, right2, right3, lane, totals, partner,
     own_sem, lane_send, lane_recv, left_send, left_recv, wrap_send,
     seed_send, seed_recv, near_send, right_recv, spread_send, sum_send, sum_recv,
 ):
     hops = nc
     items = hops * CHUNKS
     lag = CAP // LEFT
+    lefts_at, rights_at = (left0, left1, left2, left3), (right0, right1, right2, right3)
     row = lax.axis_index("row")
     c = lax.axis_index("col")
     l = lax.axis_index("layer")
@@ -62,8 +64,8 @@
 
     sibling = at(x, h, y, c, 1 - l)
 
-    own_left = pltpu.make_async_copy(left_hbm, lown.at[pl.ds(0, CAP)], own_sem.at[0])
-    own_right = pltpu.make_async_copy(right_hbm, rown, own_sem.at[1])
+    own_left = pltpu.make_async_copy(left_hbm, left0.at[pl.ds(0, CAP)], own_sem.at[0])
+    own_right = pltpu.make_async_copy(right_hbm, right0, own_sem.at[1])
     own_left.start()
     own_right.start()
 
@@ -79,8 +81,8 @@
         own_lane(0).start()
         own_lane(1).start()
 
-    lown[CAP] = jnp.zeros((BS, BS), lown.dtype)
-    lbuf[(STEPS - 1) * CAP] = jnp.zeros((BS, BS), lbuf.dtype)
+    for panel in lefts_at:
+        panel[CAP] = jnp.zeros((BS, BS), panel.dtype)
 
     barrier = pltpu.get_barrier_semaphore()
     for who in (up_prev, down_prev, sibling):
@@ -134,35 +136,55 @@
             device_id_type=MESH,
         )
 
-    def left_copy(it, src=None):
-        if src is None:
-            src = lbuf.at[pl.ds(it * LEFT, LEFT)]
-        return pltpu.make_async_remote_copy(
-            src_ref=src,
-            dst_ref=lbuf.at[pl.ds(it * LEFT, LEFT)],
-            send_sem=left_send.at[it],
-            recv_sem=left_recv.at[it],
+    def left_copy(n, step=1):
+        block = pl.ds(lax.rem(n, lag) * LEFT, LEFT)
+        return pltpu.make_async_remote_copy(
+            src_ref=lefts_at[step - 1].at[block],
+            dst_ref=lefts_at[step].at[block],
+            send_sem=left_send.at[n],
+            recv_sem=left_recv.at[n],
             device_id=on_col(jnp.maximum(c - 1, 0)),
             device_id_type=MESH,
         )
 
-    def wrap_copy(it):
-        return pltpu.make_async_remote_copy(
-            src_ref=lown.at[pl.ds(lax.rem(it, lag) * LEFT, LEFT)],
-            dst_ref=lbuf.at[pl.ds(it * LEFT, LEFT)],
-            send_sem=wrap_send.at[lax.rem(it, lag)],
-            recv_sem=left_recv.at[it],
+    def wrap_copy(n, step=1):
+        block = pl.ds(lax.rem(n, lag) * LEFT, LEFT)
+        return pltpu.make_async_remote_copy(
+            src_ref=left0.at[block],
+            dst_ref=lefts_at[step].at[block],
+            send_sem=wrap_send.at[lax.rem(n, lag)],
+            recv_sem=left_recv.at[n],
             device_id=on_col(nc - 1),
             device_id_type=MESH,
         )
+
+    def left_move(n):
+        @pl.when(n >= lag)
+        def _():
+            left_copy(n - lag).wait_recv()
+
+        for step in range(1, STEPS):
+
+            @pl.when(n // lag == step - 1)
+            def _():
+                @pl.when(c > 0)
+                def _():
+                    left_copy(n, step).start()
+
+                @pl.when(c == step - 1)
+                def _():
+                    wrap_copy(n, step).start()
+
+    def left_run(start, stop):
+        lax.fori_loop(start, stop, lambda n, _: (left_move(n), 0)[1], 0)
 
     near = 4
     near_copies = CAP // near
 
     def near_copy(s, k):
         return pltpu.make_async_remote_copy(
-            src_ref=rown.at[pl.ds(k * near, near)],
-            dst_ref=rbuf.at[pl.ds((s - 1) * CAP + k * near, near)],
+            src_ref=right0.at[pl.ds(k * near, near)],
+            dst_ref=rights_at[s].at[pl.ds(k * near, near)],
             send_sem=near_send.at[s - 1, k],
             recv_sem=right_recv.at[s - 1],
             device_id=in_group(jnp.maximum(y - s, 0)),
@@ -174,13 +196,8 @@
         for q in range(Q):
             index = (s * CB + j) * Q + q
             used = q < live_ref[s * CB + j]
-            if s == 0:
-                lefts.append(lown[jnp.where(used, lp_ref[index], CAP)])
-                rights.append(rown[rp_ref[index]])
-            else:
-                base = (s - 1) * CAP
-                lefts.append(lbuf[jnp.where(used, base + lp_ref[index], (STEPS - 1) * CAP)])
-                rights.append(rbuf[base + rp_ref[index]])
+            lefts.append(lefts_at[s][jnp.where(used, lp_ref[index], CAP)])
+            rights.append(rights_at[s][rp_ref[index]])
         return jnp.dot(
             jnp.concatenate(lefts, axis=1),
             jnp.concatenate(rights, axis=0),
@@ -188,34 +205,21 @@
         )
 
     def step(it, _):
-        @pl.when(it >= CHUNKS)
-        def _():
-            for d in range(2):
+        for d in range(2):
+
+            @pl.when(it >= CHUNKS)
+            def _():
                 lane_copy(d, it - CHUNKS).wait_recv()
 
-        @pl.when((it < CHUNKS) & (y == NY - 1))
-        def _():
-            for d in range(2):
+            @pl.when((it < CHUNKS) & (y == NY - 1))
+            def _():
                 seed(d, it).wait_recv()
 
-        for d in range(2):
             lane_copy(d, it).start()
 
-        @pl.when(it >= lag)
-        def _():
-            left_copy(it - lag).wait_recv()
-
-        @pl.when((c > 0) & (it < lag))
-        def _():
-            left_copy(it, lown.at[pl.ds(it * LEFT, LEFT)]).start()
-
-        @pl.when((c > 0) & (it >= lag))
-        def _():
-            left_copy(it, lbuf.at[pl.ds((it - lag) * LEFT, LEFT)]).start()
-
-        @pl.when(it // lag == c)
-        def _():
-            wrap_copy(it).start()
+        @pl.when(lax.rem(it, 2) == 1)
+        def _():
+            left_move(lead + it // 2)
 
         @pl.when((it >= CHUNKS) & (it < CHUNKS + near_copies))
         def _():
@@ -232,59 +236,71 @@
 
         return 0
 
+    lead = jnp.where(y == NY - 1, LEAD, 0)
+    left_run(0, lead)
     lax.fori_loop(0, items, step, 0)
 
-    def spread(d, ch, to):
-        src = jnp.where(y < NY - 1, y, ch)
+    def arrived(ch):
+        return jnp.where(y < NY - 1, y, ch)
+
+    def spread_copy(d, ch, s, to):
         block = jnp.where(y < NY - 1, (d * CHUNKS + ch) * LANE, spare + d * LANE)
-        start = (NY + src - to - 1) * CAP + block
-        return src, start
-
-    def spread_copy(d, ch, to):
-        src, start = spread(d, ch, to)
         return pltpu.make_async_remote_copy(
             src_ref=lane.at[d, pl.ds((items + ch) * LANE, LANE)],
-            dst_ref=rbuf.at[pl.ds(start, LANE)],
+            dst_ref=rights_at[s].at[pl.ds(block, LANE)],
             send_sem=spread_send.at[d, ch, to - 1],
-            recv_sem=right_recv.at[NY + src - to - 1],
+            recv_sem=right_recv.at[s - 1],
             device_id=in_group(to),
             device_id_type=MESH,
         )
 
     def spread_here(d, ch):
-        src, start = spread(d, ch, NY - 1)
         return pltpu.make_async_copy(
             lane.at[d, pl.ds((items + ch) * LANE, LANE)],
-            rbuf.at[pl.ds(start, LANE)],
-            right_recv.at[src],
-        )
-
+            rights_at[ch + 1].at[pl.ds(spare + d * LANE, LANE)],
+            right_recv.at[ch],
+        )
+
+    def each_spread(d, ch, act):
+        for to in range(1, NY):
+            for src in range(to):
+
+                @pl.when((arrived(ch) == src) & (to != y))
+                def _():
+                    act(spread_copy(d, ch, NY + src - to, to))
+
+    begun = lead + items // 2
+    left_run(begun, begun + 4)
     for ch in range(CHUNKS):
         for d in range(2):
             lane_copy(d, items - CHUNKS + ch).wait_recv()
-            for to in range(1, NY):
-                src, _ = spread(d, ch, to)
-
-                @pl.when((to > src) & (to != y))
-                def _():
-                    spread_copy(d, ch, to).start()
+            each_spread(d, ch, lambda copy: copy.start())
 
             @pl.when(y == NY - 1)
             def _():
                 spread_here(d, ch).start()
 
-    lax.fori_loop(items - lag, items, lambda it, _: (left_copy(it).wait_recv(), 0)[1], 0)
-    for s in range(1, STEPS):
-        panel = rbuf.at[pl.ds((s - 1) * CAP, CAP)]
-        pltpu.make_async_copy(panel, panel, right_recv.at[s - 1]).wait()
+        left_run(begun + 4 + 2 * ch, begun + 6 + 2 * ch)
+    left_run(begun + 10, items)
+
+    def right_wait(s):
+        pltpu.make_async_copy(rights_at[s], rights_at[s], right_recv.at[s - 1]).wait()
+
+    right_wait(1)
+    right_wait(2)
+
+    def middle(j, _):
+        totals[j] = totals[j] + (pair_sum(j, 1) + pair_sum(j, 2))
+        return 0
+
+    lax.fori_loop(0, CB, middle, 0)
+    right_wait(3)
+    lax.fori_loop(items - lag, items, lambda n, _: (left_copy(n).wait_recv(), 0)[1], 0)
 
     half = CB // 2
 
     def rest(j):
-        total = totals[j]
-        for s in range(1, STEPS):
-            total = total + pair_sum(j, s)
-        return total
+        return totals[j] + pair_sum(j, 3)
 
     def sum_copy(i):
         return pltpu.make_async_remote_copy(
@@ -338,12 +354,7 @@
 
     for ch in range(CHUNKS):
         for d in range(2):
-            for to in range(1, NY):
-                src, _ = spread(d, ch, to)
-
-                @pl.when((to > src) & (to != y))
-                def _():
-                    spread_copy(d, ch, to).wait_send()
+            each_spread(d, ch, lambda copy: copy.wait_send())
 
     def finish(i, _):
         sum_copy(i).wait_recv()
@@ -368,10 +379,8 @@
             + [pl.BlockSpec(memory_space=pl.ANY)] * 2,
             out_specs=pl.BlockSpec(memory_space=pltpu.VMEM),
             scratch_shapes=[
-                pltpu.VMEM((CAP + 1, BS, BS), jnp.bfloat16),
-                pltpu.VMEM((CAP, BS, BS), jnp.bfloat16),
-                pltpu.VMEM(((STEPS - 1) * CAP + 1, BS, BS), jnp.bfloat16),
-                pltpu.VMEM(((STEPS - 1) * CAP, BS, BS), jnp.bfloat16),
+                *[pltpu.VMEM((CAP + 1, BS, BS), jnp.bfloat16)] * STEPS,
+                *[pltpu.VMEM((CAP, BS, BS), jnp.bfloat16)] * STEPS,
                 pltpu.VMEM((2, (items + CHUNKS) * LANE, BS, BS), jnp.bfloat16),
                 pltpu.VMEM((CB, BS, BS), jnp.float32),
                 pltpu.VMEM((CB // 2, BS, BS), jnp.float32),
@@ -390,7 +399,7 @@
                 dma((CB // 2,)),
             ],
             compiler_params=pltpu.CompilerParams(
-                collective_id=0, has_side_effects=True, vmem_limit_bytes=48 * 2**20
+                collective_id=0, has_side_effects=True, vmem_limit_bytes=60 * 2**20
             ),
             name="cannon_window",
         )(

time: 266 us -> 244 us (0.917)
  the two profiles are of different devices: /device:TPU:116 before, /device:TPU:1 now
where the time goes in v2:
time: 244 us; the launch traced here: 243 us
  Pallas kernels  237 us (97%)
  local copies, waits for them, and re-layouts  5.45 us (2%)
    pallas_call x1, Pallas kernels, local(): pl.pallas_call(functools.partial(kernel, nx, nc), out_shape=jax.ShapeDtyp...  237 us

profile of v2, /device:TPU:1, one launch (start us, length us, event | category | flops | bytes accessed | tf_op | source)
XLA Modules:
  0.0 242.9 jit_solution(9351586437479382880)
XLA Ops:
  0.0 0.0 copy-start.1
  0.0 0.7 copy-done.1
  0.7 0.6 reshape.11.live_ref
  1.3 0.8 copy.6
  2.1 0.0 copy-start
  2.1 0.7 reshape.9.lp_ref
  2.8 0.0 copy-done
  2.8 0.1 copy.7
  2.9 0.7 reshape.10.rp_ref
  3.6 237.4 %cannon_window.1 = f32[8,128,128]{2,1,0:T(8,128)} custom-call(s32[256]{0:T(256)} %reshape.9.lp_ref, s32[256]{0:T(256)} %reshape.10.rp_ref, s32[64]{0:T(128)} %reshape.11.live_ref, bf16[32,128,128]{2,1,0:T(8,128)(2,1)} %bitcast.8, bf16[32,128,128]{2,1,0:T(8,128)(2,1)} %bitcast.9), custom_call_target="tpu_custom_call" | custom-call | tf_op jit(solution)/shard_map/cannon_window/pallas_call | solution.py:375
  241.0 1.9 copy.9
Async XLA Ops:
  0.0 0.7 copy-start.1
  2.1 0.7 copy-start

commit v3 on v2

--- a/solution.py
+++ b/solution.py
@@ -23,9 +23,9 @@
 
 def kernel(
     nx, nc,
-    lp_ref, rp_ref, live_ref, left_hbm, right_hbm, out_ref,
-    left0, left1, left2, left3, right0, right1, right2, right3, lane, totals, partner,
-    own_sem, lane_send, lane_recv, left_send, left_recv, wrap_send,
+    lp_hbm, rp_hbm, live_hbm, left_hbm, right_hbm, out_ref, partner,
+    lp_ref, rp_ref, live_ref, left0, left1, left2, left3, right0, right1, right2, right3, lane, totals,
+    own_sem, list_sem, lane_send, lane_recv, left_send, left_recv, wrap_send,
     seed_send, seed_recv, near_send, right_recv, spread_send, sum_send, sum_recv,
 ):
     hops = nc
@@ -68,6 +68,12 @@
     own_right = pltpu.make_async_copy(right_hbm, right0, own_sem.at[1])
     own_left.start()
     own_right.start()
+    lists = [
+        pltpu.make_async_copy(src, dst, list_sem.at[i])
+        for i, (src, dst) in enumerate(((lp_hbm, lp_ref), (rp_hbm, rp_ref), (live_hbm, live_ref)))
+    ]
+    for copy in lists:
+        copy.start()
 
     def own_lane(d):
         return pltpu.make_async_copy(
@@ -125,6 +131,8 @@
 
     own_left.wait()
     own_right.wait()
+    for copy in lists:
+        copy.wait()
 
     def lane_copy(d, it):
         return pltpu.make_async_remote_copy(
@@ -194,10 +202,9 @@
     def pair_sum(j, s):
         lefts, rights = [], []
         for q in range(Q):
-            index = (s * CB + j) * Q + q
-            used = q < live_ref[s * CB + j]
-            lefts.append(lefts_at[s][jnp.where(used, lp_ref[index], CAP)])
-            rights.append(rights_at[s][rp_ref[index]])
+            used = q < live_ref[s, j]
+            lefts.append(lefts_at[s][jnp.where(used, lp_ref[s, q, j], CAP)])
+            rights.append(rights_at[s][rp_ref[s, q, j]])
         return jnp.dot(
             jnp.concatenate(lefts, axis=1),
             jnp.concatenate(rights, axis=0),
@@ -286,6 +293,33 @@
     def right_wait(s):
         pltpu.make_async_copy(rights_at[s], rights_at[s], right_recv.at[s - 1]).wait()
 
+    def lanes_gone(it, _):
+        for d in range(2):
+            lane_copy(d, it).wait_send()
+
+        @pl.when((c > 0) & (it < items - lag))
+        def _():
+            left_copy(it).wait_send()
+
+        @pl.when(it // lag == c)
+        def _():
+            wrap_copy(it).wait_send()
+
+        return 0
+
+    lax.fori_loop(0, items, lanes_gone, 0)
+
+    @pl.when(y < NY - 1)
+    def _():
+        seed(0, y).wait_send()
+        seed(1, y).wait_send()
+
+    for s in range(1, STEPS):
+
+        @pl.when(y >= s)
+        def _():
+            lax.fori_loop(0, near_copies, lambda k, _: (near_copy(s, k).wait_send(), 0)[1], 0)
+
     right_wait(1)
     right_wait(2)
 
@@ -295,6 +329,10 @@
 
     lax.fori_loop(0, CB, middle, 0)
     right_wait(3)
+    for ch in range(CHUNKS):
+        for d in range(2):
+            each_spread(d, ch, lambda copy: copy.wait_send())
+
     lax.fori_loop(items - lag, items, lambda n, _: (left_copy(n).wait_recv(), 0)[1], 0)
 
     half = CB // 2
@@ -325,42 +363,14 @@
     lax.fori_loop(0, half, theirs, 0)
     lax.fori_loop(0, half, ours, 0)
 
-    def lanes_gone(it, _):
-        for d in range(2):
-            lane_copy(d, it).wait_send()
-
-        @pl.when(c > 0)
-        def _():
-            left_copy(it).wait_send()
-
-        @pl.when(it // lag == c)
-        def _():
-            wrap_copy(it).wait_send()
-
-        return 0
-
-    lax.fori_loop(0, items, lanes_gone, 0)
-
-    @pl.when(y < NY - 1)
-    def _():
-        seed(0, y).wait_send()
-        seed(1, y).wait_send()
-
-    for s in range(1, STEPS):
-
-        @pl.when(y >= s)
-        def _():
-            lax.fori_loop(0, near_copies, lambda k, _: (near_copy(s, k).wait_send(), 0)[1], 0)
-
-    for ch in range(CHUNKS):
-        for d in range(2):
-            each_spread(d, ch, lambda copy: copy.wait_send())
-
     def finish(i, _):
         sum_copy(i).wait_recv()
-        out_ref[i] = out_ref[i] + partner[i]
         sum_copy(i).wait_send()
         return 0
+
+    @pl.when(c > 0)
+    def _():
+        lax.fori_loop(items - lag, items, lambda n, _: (left_copy(n).wait_send(), 0)[1], 0)
 
     lax.fori_loop(0, half, finish, 0)
 
@@ -372,19 +382,21 @@
     dma = pltpu.SemaphoreType.DMA
 
     def local(left_panels, right_panels, left_picks, right_picks, live_count):
-        summed = pl.pallas_call(
+        own, partner = pl.pallas_call(
             functools.partial(kernel, nx, nc),
-            out_shape=jax.ShapeDtypeStruct((CB // 2, BS, BS), jnp.float32),
-            in_specs=[pl.BlockSpec(memory_space=pltpu.SMEM)] * 3
-            + [pl.BlockSpec(memory_space=pl.ANY)] * 2,
-            out_specs=pl.BlockSpec(memory_space=pltpu.VMEM),
+            out_shape=[jax.ShapeDtypeStruct((CB // 2, BS, BS), jnp.float32)] * 2,
+            in_specs=[pl.BlockSpec(memory_space=pltpu.HBM)] * 5,
+            out_specs=[pl.BlockSpec(memory_space=pltpu.VMEM)] * 2,
             scratch_shapes=[
+                pltpu.SMEM((STEPS, Q, CB), jnp.int32),
+                pltpu.SMEM((STEPS, Q, CB), jnp.int32),
+                pltpu.SMEM((STEPS, CB), jnp.int32),
                 *[pltpu.VMEM((CAP + 1, BS, BS), jnp.bfloat16)] * STEPS,
                 *[pltpu.VMEM((CAP, BS, BS), jnp.bfloat16)] * STEPS,
                 pltpu.VMEM((2, (items + CHUNKS) * LANE, BS, BS), jnp.bfloat16),
                 pltpu.VMEM((CB, BS, BS), jnp.float32),
-                pltpu.VMEM((CB // 2, BS, BS), jnp.float32),
                 dma((4,)),
+                dma((3,)),
                 dma((2, items)),
                 dma((2, items)),
                 dma((items,)),
@@ -403,13 +415,13 @@
             ),
             name="cannon_window",
         )(
-            left_picks.reshape(-1),
-            right_picks.reshape(-1),
-            live_count.reshape(-1),
+            jnp.swapaxes(left_picks[0, 0, 0], 1, 2),
+            jnp.swapaxes(right_picks[0, 0, 0], 1, 2),
+            live_count[0, 0, 0],
             left_panels[0, 0, 0],
             right_panels[0, 0, 0],
         )
-        return summed[None, None]
+        return (own + partner)[None, None]
 
     placed = (
         P("row", "col", "layer", None, None, None),

time: 244 us -> 240 us (0.984)
  local copies, waits for them, and re-layouts: 5.45 us -> 0 us
    unnamed x7 -> x0, local copies, waits for them, and re-layouts: 3.47 us -> none
where the time goes in v3:
time: 240 us; the launch traced here: 239 us
  Pallas kernels  237 us (99%)
    pallas_call x1, Pallas kernels, local(): pl.pallas_call(functools.partial(kernel, nx, nc), out_shape=[jax.ShapeDty...  237 us

profile of v3, /device:TPU:1, one launch (start us, length us, event | category | flops | bytes accessed | tf_op | source)
XLA Modules:
  0.0 238.8 jit_solution(11459568692079097810)
XLA Ops:
  0.0 236.7 %cannon_window.1 = (f32[8,128,128]{2,1,0:T(8,128)}, f32[8,128,128]{2,1,0:T(8,128)}) custom-call(s32[4,4,16]{2,1,0:T(4,128)} %bitcast.13, s32[4,4,16]{2,1,0:T(4,128)} %bitcast.14, s32[4,16]{1,0:T(4,128)} %bitcast.15, bf16[32,128,128]{2,1,0:T(8,128)(2,1)} %bitcast.11, bf16[32,128,128]{2,1,0:T(8,128)(2,1)} %bitcast.12), custom_call_target="tpu_custom_call" | custom-call | tf_op jit(solution)/shard_map/cannon_window/pallas_call | solution.py:385
  236.7 2.0 add_bitcast_fusion

commit v4 on v3

--- a/solution.py
+++ b/solution.py
@@ -18,6 +18,8 @@
 CHUNKS = 3
 LANE = 4
 LEFT = 2
+UNROLL = 4
+AHEAD = 16
 LEAD = 8
 
 
@@ -27,6 +29,7 @@
     lp_ref, rp_ref, live_ref, left0, left1, left2, left3, right0, right1, right2, right3, lane, totals,
     own_sem, list_sem, lane_send, lane_recv, left_send, left_recv, wrap_send,
     seed_send, seed_recv, near_send, right_recv, spread_send, sum_send, sum_recv,
+    down_ready, wrap_ready,
 ):
     hops = nc
     items = hops * CHUNKS
@@ -64,6 +67,30 @@
 
     sibling = at(x, h, y, c, 1 - l)
 
+    barrier = pltpu.get_barrier_semaphore()
+    def greet(who):
+        pl.semaphore_signal(barrier, inc=1, device_id=who, device_id_type=MESH)
+
+    greet(up_prev)
+    greet(sibling)
+    for k in range(1, NY):
+        greet(in_group(lax.rem(y + k, NY)))
+
+    @pl.when(c < nc - 1)
+    def _():
+        greet(down_prev)
+        greet(on_col(c + 1))
+
+    @pl.when(first)
+    def _():
+        greet(down_next)
+
+    @pl.when(c < STEPS - 1)
+    def _():
+        greet(on_col(nc - 1))
+
+    greeted = 2 + (NY - 1) + jnp.where(c > 0, 2, 0) + jnp.where(last, STEPS, 0)
+
     own_left = pltpu.make_async_copy(left_hbm, left0.at[pl.ds(0, CAP)], own_sem.at[0])
     own_right = pltpu.make_async_copy(right_hbm, right0, own_sem.at[1])
     own_left.start()
@@ -75,40 +102,16 @@
     for copy in lists:
         copy.start()
 
-    def own_lane(d):
-        return pltpu.make_async_copy(
-            right_hbm.at[pl.ds(d * CHUNKS * LANE, CHUNKS * LANE)],
-            lane.at[d, pl.ds(0, CHUNKS * LANE)],
-            own_sem.at[2 + d],
-        )
-
-    @pl.when(y < NY - 1)
-    def _():
-        own_lane(0).start()
-        own_lane(1).start()
-
     for panel in lefts_at:
         panel[CAP] = jnp.zeros((BS, BS), panel.dtype)
 
-    barrier = pltpu.get_barrier_semaphore()
-    for who in (up_prev, down_prev, sibling):
-        pl.semaphore_signal(barrier, inc=1, device_id=who, device_id_type=MESH)
-    for k in range(1, NY):
-        pl.semaphore_signal(
-            barrier, inc=1, device_id=in_group(lax.rem(y + k, NY)), device_id_type=MESH
-        )
-
-    @pl.when(c < nc - 1)
-    def _():
-        pl.semaphore_signal(barrier, inc=1, device_id=on_col(c + 1), device_id_type=MESH)
+    pl.semaphore_wait(barrier, greeted)
 
     @pl.when(last)
     def _():
+        pl.semaphore_signal(down_ready, inc=1, device_id=down_prev, device_id_type=MESH)
         for k in range(STEPS - 1):
-            pl.semaphore_signal(barrier, inc=1, device_id=on_col(k), device_id_type=MESH)
-
-    greeted = 3 + (NY - 1) + jnp.where(c > 0, 1, 0) + jnp.where(c < STEPS - 1, 1, 0)
-    pl.semaphore_wait(barrier, greeted)
+            pl.semaphore_signal(wrap_ready, inc=1, device_id=on_col(k), device_id_type=MESH)
 
     spare = 2 * CHUNKS * LANE
 
@@ -126,17 +129,11 @@
     def _():
         seed(0, y).start()
         seed(1, y).start()
-        own_lane(0).wait()
-        own_lane(1).wait()
-
-    own_left.wait()
-    own_right.wait()
-    for copy in lists:
-        copy.wait()
-
-    def lane_copy(d, it):
-        return pltpu.make_async_remote_copy(
-            src_ref=lane.at[d, pl.ds(it * LANE, LANE)],
+
+
+    def lane_copy(d, it, src=None):
+        return pltpu.make_async_remote_copy(
+            src_ref=lane.at[d, pl.ds(it * LANE, LANE)] if src is None else src,
             dst_ref=lane.at[d, pl.ds((it + CHUNKS) * LANE, LANE)],
             send_sem=lane_send.at[d, it],
             recv_sem=lane_recv.at[d, it],
@@ -147,7 +144,7 @@
     def left_copy(n, step=1):
         block = pl.ds(lax.rem(n, lag) * LEFT, LEFT)
         return pltpu.make_async_remote_copy(
-            src_ref=lefts_at[step - 1].at[block],
+            src_ref=(left_hbm if step == 1 else lefts_at[step - 1]).at[block],
             dst_ref=lefts_at[step].at[block],
             send_sem=left_send.at[n],
             recv_sem=left_recv.at[n],
@@ -158,7 +155,7 @@
     def wrap_copy(n, step=1):
         block = pl.ds(lax.rem(n, lag) * LEFT, LEFT)
         return pltpu.make_async_remote_copy(
-            src_ref=left0.at[block],
+            src_ref=left_hbm.at[block],
             dst_ref=lefts_at[step].at[block],
             send_sem=wrap_send.at[lax.rem(n, lag)],
             recv_sem=left_recv.at[n],
@@ -179,9 +176,21 @@
                 def _():
                     left_copy(n, step).start()
 
-                @pl.when(c == step - 1)
-                def _():
-                    wrap_copy(n, step).start()
+    def wrap_move(n):
+        @pl.when(n == c * lag)
+        def _():
+            pl.semaphore_wait(wrap_ready, 1)
+
+        for step in range(1, STEPS):
+
+            @pl.when((n // lag == step - 1) & (c == step - 1))
+            def _():
+                wrap_copy(n, step).start()
+
+    def wrap_run(start, stop):
+        @pl.when(c < STEPS - 1)
+        def _():
+            lax.fori_loop(start, stop, lambda n, _: (wrap_move(n), 0)[1], 0)
 
     def left_run(start, stop):
         lax.fori_loop(start, stop, lambda n, _: (left_move(n), 0)[1], 0)
@@ -191,7 +200,7 @@
 
     def near_copy(s, k):
         return pltpu.make_async_remote_copy(
-            src_ref=right0.at[pl.ds(k * near, near)],
+            src_ref=right_hbm.at[pl.ds(k * near, near)],
             dst_ref=rights_at[s].at[pl.ds(k * near, near)],
             send_sem=near_send.at[s - 1, k],
             recv_sem=right_recv.at[s - 1],
@@ -211,22 +220,48 @@
             preferred_element_type=jnp.float32,
         )
 
+    def lane_move(d, k):
+        @pl.when(k >= CHUNKS)
+        def _():
+            lane_copy(d, k - CHUNKS).wait_recv()
+
+        @pl.when((k < CHUNKS) & (y == NY - 1))
+        def _():
+            seed(d, k).wait_recv()
+
+        @pl.when((k < CHUNKS) & (y < NY - 1))
+        def _():
+            lane_copy(d, k, right_hbm.at[pl.ds((d * CHUNKS + k) * LANE, LANE)]).start()
+
+        @pl.when((k >= CHUNKS) | (y == NY - 1))
+        def _():
+            lane_copy(d, k).start()
+
+    ahead = jnp.where((h == 0) & (c > 0) & (y < NY - 1), jnp.maximum(AHEAD - c, 0) // 4, 0)
+
+    lead = jnp.where(y == NY - 1, LEAD, 0)
     def step(it, _):
-        for d in range(2):
-
-            @pl.when(it >= CHUNKS)
+        up = it - ahead
+
+        @pl.when(up >= CHUNKS)
+        def _():
+            lane_move(0, up)
+
+        @pl.when((it == 0) & first)
+        def _():
+            pl.semaphore_wait(down_ready, 1)
+
+        @pl.when(it < items)
+        def _():
+            lane_move(1, it)
+
+        @pl.when((lax.rem(it, 2) == 1) & (it < items))
+        def _():
+            left_move(lead + it // 2)
+
+            @pl.when(c < STEPS - 1)
             def _():
-                lane_copy(d, it - CHUNKS).wait_recv()
-
-            @pl.when((it < CHUNKS) & (y == NY - 1))
-            def _():
-                seed(d, it).wait_recv()
-
-            lane_copy(d, it).start()
-
-        @pl.when(lax.rem(it, 2) == 1)
-        def _():
-            left_move(lead + it // 2)
+                wrap_move(it // 2)
 
         @pl.when((it >= CHUNKS) & (it < CHUNKS + near_copies))
         def _():
@@ -236,16 +271,21 @@
                 def _():
                     near_copy(s, it - CHUNKS).start()
 
-        @pl.when(lax.rem(it, CHUNKS) == 2)
+        @pl.when((lax.rem(it, CHUNKS) == 2) & (it < items))
         def _():
             j = it // CHUNKS
             totals[j] = pair_sum(j, 0)
 
         return 0
 
-    lead = jnp.where(y == NY - 1, LEAD, 0)
     left_run(0, lead)
-    lax.fori_loop(0, items, step, 0)
+    for k in range(CHUNKS):
+        lane_move(0, k)
+    own_left.wait()
+    own_right.wait()
+    for copy in lists:
+        copy.wait()
+    lax.fori_loop(0, items + ahead, step, 0)
 
     def arrived(ch):
         return jnp.where(y < NY - 1, y, ch)
@@ -277,6 +317,7 @@
                     act(spread_copy(d, ch, NY + src - to, to))
 
     begun = lead + items // 2
+    wrap_run(items // 2, items)
     left_run(begun, begun + 4)
     for ch in range(CHUNKS):
         for d in range(2):
@@ -301,10 +342,6 @@
         def _():
             left_copy(it).wait_send()
 
-        @pl.when(it // lag == c)
-        def _():
-            wrap_copy(it).wait_send()
-
         return 0
 
     lax.fori_loop(0, items, lanes_gone, 0)
@@ -327,7 +364,7 @@
         totals[j] = totals[j] + (pair_sum(j, 1) + pair_sum(j, 2))
         return 0
 
-    lax.fori_loop(0, CB, middle, 0)
+    lax.fori_loop(0, CB, middle, 0, unroll=UNROLL)
     right_wait(3)
     for ch in range(CHUNKS):
         for d in range(2):
@@ -360,8 +397,8 @@
         out_ref[i] = rest(l * half + i)
         return 0
 
-    lax.fori_loop(0, half, theirs, 0)
-    lax.fori_loop(0, half, ours, 0)
+    lax.fori_loop(0, half, theirs, 0, unroll=UNROLL)
+    lax.fori_loop(0, half, ours, 0, unroll=UNROLL)
 
     def finish(i, _):
         sum_copy(i).wait_recv()
@@ -371,6 +408,10 @@
     @pl.when(c > 0)
     def _():
         lax.fori_loop(items - lag, items, lambda n, _: (left_copy(n).wait_send(), 0)[1], 0)
+
+    @pl.when(c < STEPS - 1)
+    def _():
+        lax.fori_loop(0, lag, lambda n, _: (wrap_copy(n).wait_send(), 0)[1], 0)
 
     lax.fori_loop(0, half, finish, 0)
 
@@ -395,7 +436,7 @@
                 *[pltpu.VMEM((CAP, BS, BS), jnp.bfloat16)] * STEPS,
                 pltpu.VMEM((2, (items + CHUNKS) * LANE, BS, BS), jnp.bfloat16),
                 pltpu.VMEM((CB, BS, BS), jnp.float32),
-                dma((4,)),
+                dma((2,)),
                 dma((3,)),
                 dma((2, items)),
                 dma((2, items)),
@@ -409,6 +450,8 @@
                 dma((2, CHUNKS, NY - 1)),
                 dma((CB // 2,)),
                 dma((CB // 2,)),
+                pltpu.SemaphoreType.REGULAR,
+                pltpu.SemaphoreType.REGULAR,
             ],
             compiler_params=pltpu.CompilerParams(
                 collective_id=0, has_side_effects=True, vmem_limit_bytes=60 * 2**20

time: 240 us -> 236 us (0.983)
  the two profiles are of different devices: /device:TPU:1 before, /device:TPU:1023 now
where the time goes in v4:
time: 236 us
  Pallas kernels  233 us (99%)
    pallas_call x1, Pallas kernels, local(): pl.pallas_call(functools.partial(kernel, nx, nc), out_shape=[jax.ShapeDty...  233 us

profile of v4, /device:TPU:1023, one launch (start us, length us, event | category | flops | bytes accessed | tf_op | source)
XLA Modules:
  0.0 235.5 jit_solution(9819837970522732306)
XLA Ops:
  0.0 233.4 %cannon_window.1 = (f32[8,128,128]{2,1,0:T(8,128)}, f32[8,128,128]{2,1,0:T(8,128)}) custom-call(s32[4,4,16]{2,1,0:T(4,128)} %bitcast.13, s32[4,4,16]{2,1,0:T(4,128)} %bitcast.14, s32[4,16]{1,0:T(4,128)} %bitcast.15, bf16[32,128,128]{2,1,0:T(8,128)(2,1)} %bitcast.11, bf16[32,128,128]{2,1,0:T(8,128)(2,1)} %bitcast.12), custom_call_target="tpu_custom_call" | custom-call | tf_op jit(solution)/shard_map/cannon_window/pallas_call | solution.py:426
  233.5 2.0 add_bitcast_fusion
